TPU v7x, 32 devices: a whole 2x2x4 slice. The times are simulated.
32 devices in a mesh: dp: 8 (over z, x), tensor: 4 (over y, core).
Axes of the slice: x: 2, y: 2, z: 4, core: 2. Of those that a mesh axis runs over, the one named last changes fastest.
Arguments:
- tokens: bfloat16 [10976, 1280], P(('dp', 'tensor')), may hold values from -6 to 6
- grad_out: bfloat16 [10976, 1280], P(('dp', 'tensor')), may hold values from -6 to 6
- adapter_index: int32 [2], replicated, may hold values from 0 to 7
- norm1_gain: bfloat16 [1280], replicated, may hold values from 0.099609375 to 1.8984375
- norm1_shift: bfloat16 [1280], replicated, may hold values from -2.5 to 2.5
- qkv_weight: bfloat16 [1280, 3, 1280], P(None, None, 'tensor'), may hold values from -0.15625 to 0.15625
- qkv_bias: bfloat16 [3, 1280], P(None, 'tensor'), may hold values from -2.5 to 2.5
- rel_pos_h: bfloat16 [27, 80], replicated, may hold values from -1.25 to 1.25
- rel_pos_w: bfloat16 [27, 80], replicated, may hold values from -1.25 to 1.25
- proj_weight: bfloat16 [1280, 1280], P('tensor'), may hold values from -0.625 to 0.625
- proj_bias: bfloat16 [1280], replicated, may hold values from -2.5 to 2.5
- norm2_gain: bfloat16 [1280], replicated, may hold values from 0.099609375 to 1.8984375
- norm2_shift: bfloat16 [1280], replicated, may hold values from -2.5 to 2.5
- lin1_weight: bfloat16 [1280, 5120], P(None, 'tensor'), may hold values from -0.15625 to 0.15625
- lin1_bias: bfloat16 [5120], P('tensor'), may hold values from -2.5 to 2.5
- lin2_weight: bfloat16 [5120, 1280], P('tensor'), may hold values from -0.078125 to 0.078125
- lin2_bias: bfloat16 [1280], replicated, may hold values from -2.5 to 2.5
- qkv_down: bfloat16 [8, 1280, 16], replicated, may hold values from -0.15625 to 0.15625
- qkv_up: bfloat16 [8, 16, 3, 1280], P(None, None, None, 'tensor'), may hold values from -1.5 to 1.5
- proj_down: bfloat16 [8, 1280, 16], P(None, 'tensor'), may hold values from -0.625 to 0.625
- proj_up: bfloat16 [8, 16, 1280], replicated, may hold values from -1.5 to 1.5
- lin1_down: bfloat16 [8, 1280, 16], replicated, may hold values from -0.15625 to 0.15625
- lin1_up: bfloat16 [8, 16, 5120], P(None, None, 'tensor'), may hold values from -1.5 to 1.5
- lin2_down: bfloat16 [8, 5120, 16], P(None, 'tensor'), may hold values from -0.078125 to 0.078125
- lin2_up: bfloat16 [8, 16, 1280], replicated, may hold values from -1.5 to 1.5
Outputs:
- output: bfloat16 [10976, 1280], P(('dp', 'tensor'))
- grad_tokens: bfloat16 [10976, 1280], P(('dp', 'tensor'))
- grad_qkv_down: float32 [8, 1280, 16], replicated
- grad_qkv_up: float32 [8, 16, 3, 1280], P(None, None, None, 'tensor')
- grad_proj_down: float32 [8, 1280, 16], P(None, 'tensor')
- grad_proj_up: float32 [8, 16, 1280], replicated
- grad_lin1_down: float32 [8, 1280, 16], replicated
- grad_lin1_up: float32 [8, 16, 5120], P(None, None, 'tensor')
- grad_lin2_down: float32 [8, 5120, 16], P(None, 'tensor')
- grad_lin2_up: float32 [8, 16, 1280], replicated
Inputs may be any that keep to these rules, and one draw needn't show every extreme that they name: `adapter_index`: one adapter for each image.
All inputs are finite; a program needn't handle non-finite values.
Results may differ from a plain program's by a relative error of at most 0.019.
Values may be sent and summed in bfloat16 or wider, within the bound.
A program may use at most 256 MiB of HBM per device.

v0:
```python
import jax
import jax.numpy as jnp
from jax import lax
from jax.sharding import PartitionSpec as P

HEAD_DIM = 80
WIN = 14
SIDE = 64
RANK = 16
ADAPTERS = 8
WIN_DEV = 7
GROUP = 4
GRID = 5
HIGH = lax.Precision.HIGHEST
ADAPT = 0.5
EPS = 1e-06


def fast_dot(first_op, second_op):
    return jnp.dot(first_op, second_op, preferred_element_type=jnp.float32)


def trans_dot(first_op, second_op):
    return lax.dot_general(
        first_op, second_op, (((1,), (1,)), ((), ())), preferred_element_type=jnp.float32
    )


def exact_dot(first_op, second_op):
    return jnp.dot(first_op, second_op.astype(jnp.float32), precision=HIGH)


def cross_dot(first_op, second_op):
    return lax.dot_general(
        first_op.astype(jnp.float32),
        second_op.astype(jnp.float32),
        (((0,), (0,)), ((), ())),
        precision=HIGH,
    )


def window_mask(first_slot, count_all):
    position = jnp.arange(count_all, dtype=jnp.int32)
    slot_index = first_slot + position // (WIN * WIN)
    within = position % (WIN * WIN)
    image_row = slot_index // GRID * WIN + within // WIN
    image_col = slot_index % GRID * WIN + within % WIN
    inside = (slot_index < GRID * GRID) & (image_row < SIDE) & (image_col < SIDE)
    return jnp.where(inside, 1.0, 0.0).astype(jnp.float32)[:, None]


def offset_table(position_table):
    offsets = (jnp.arange(WIN)[:, None] - jnp.arange(WIN)[None, :] + WIN - 1).reshape(-1)
    one_hot = (offsets[:, None] == jnp.arange(2 * WIN - 1)[None, :]).astype(jnp.float32)
    return exact_dot(one_hot, position_table).reshape(WIN, WIN, -1).astype(jnp.bfloat16)


def norm_parts(values):
    row_mean = jnp.mean(values, axis=-1, keepdims=True)
    centered = values - row_mean
    inv_std = lax.rsqrt(jnp.mean(centered * centered, axis=-1, keepdims=True) + EPS)
    return (centered * inv_std, inv_std)


def norm_back(grad_in, normalized, inv_std, norm_gain):
    scaled = grad_in * norm_gain
    return inv_std * (
        scaled
        - jnp.mean(scaled, axis=-1, keepdims=True)
        - normalized * jnp.mean(scaled * normalized, axis=-1, keepdims=True)
    )


def window_scores(queries, key_win, table_h, table_w):
    win_count, head_count = (queries.shape[0], queries.shape[1])
    tokens_win = WIN * WIN
    base_scores = jnp.einsum(
        "nhqc,nhkc->nhqk",
        queries.reshape(win_count, head_count, tokens_win, -1),
        key_win.reshape(win_count, head_count, tokens_win, -1),
        preferred_element_type=jnp.float32,
    ) * HEAD_DIM ** (-0.5)
    rel_rows = jnp.einsum("nhabc,akc->nhabk", queries, table_h, preferred_element_type=jnp.float32)
    rel_cols = jnp.einsum("nhabc,bkc->nhabk", queries, table_w, preferred_element_type=jnp.float32)
    scores = (
        base_scores.reshape(win_count, head_count, WIN, WIN, WIN, WIN)
        + rel_rows[:, :, :, :, :, None]
        + rel_cols[:, :, :, :, None, :]
    )
    return scores.reshape(win_count, head_count, tokens_win, tokens_win)


def attention_back(queries, key_win, value_win, log_total, grad_att, table_h, table_w):
    win_count, head_count = (queries.shape[0], queries.shape[1])
    tokens_win = WIN * WIN
    probs = jnp.exp(window_scores(queries, key_win, table_h, table_w) - log_total)
    grad_rows = grad_att.reshape(win_count, head_count, tokens_win, -1)
    dprob = jnp.einsum(
        "nhqc,nhkc->nhqk",
        grad_rows,
        value_win.reshape(win_count, head_count, tokens_win, -1),
        preferred_element_type=jnp.float32,
    )
    dvalues = jnp.einsum(
        "nhqk,nhqc->nhkc", probs.astype(jnp.bfloat16), grad_rows, preferred_element_type=jnp.float32
    )
    inner_sum = jnp.sum(probs * dprob, axis=-1, keepdims=True)
    dscore = (probs * (dprob - inner_sum)).astype(jnp.bfloat16)
    dqueries = jnp.einsum(
        "nhqk,nhkc->nhqc",
        dscore,
        key_win.reshape(win_count, head_count, tokens_win, -1),
        preferred_element_type=jnp.float32,
    ) * HEAD_DIM ** (-0.5)
    dkeys = jnp.einsum(
        "nhqk,nhqc->nhkc",
        dscore,
        queries.reshape(win_count, head_count, tokens_win, -1),
        preferred_element_type=jnp.float32,
    ) * HEAD_DIM ** (-0.5)
    dscore_six = dscore.astype(jnp.float32).reshape(win_count, head_count, WIN, WIN, WIN, WIN)
    from_rows = jnp.einsum(
        "nhabk,akc->nhabc", jnp.sum(dscore_six, axis=5), table_h.astype(jnp.float32), precision=HIGH
    )
    from_cols = jnp.einsum(
        "nhabk,bkc->nhabc", jnp.sum(dscore_six, axis=4), table_w.astype(jnp.float32), precision=HIGH
    )
    dqueries = dqueries.reshape(queries.shape) + from_rows + from_cols
    return (
        dqueries.astype(jnp.bfloat16),
        dkeys.reshape(queries.shape).astype(jnp.bfloat16),
        dvalues.reshape(queries.shape).astype(jnp.bfloat16),
    )


def on_device(
    tokens,
    grad_out,
    adapter_index,
    norm1_gain,
    norm1_shift,
    qkv_weight,
    qkv_bias,
    rel_pos_h,
    rel_pos_w,
    proj_weight,
    proj_bias,
    norm2_gain,
    norm2_shift,
    lin1_weight,
    lin1_bias,
    lin2_weight,
    lin2_bias,
    qkv_down,
    qkv_up,
    proj_down,
    proj_up,
    lin1_down,
    lin1_up,
    lin2_down,
    lin2_up,
):
    tensor_size = lax.axis_size("tensor")
    row_count = tokens.shape[0]
    full_rows = row_count * tensor_size
    dp_place = lax.axis_index("dp")
    tensor_place = lax.axis_index("tensor")
    valid_full = window_mask(dp_place % GROUP * WIN_DEV, full_rows)
    valid_local = lax.dynamic_slice_in_dim(valid_full, tensor_place * row_count, row_count, 0)
    image_place = dp_place // GROUP
    pick = jnp.sum(jnp.where(jnp.arange(adapter_index.shape[0]) == image_place, adapter_index, 0))
    slot_hot = jnp.where(jnp.arange(ADAPTERS) == pick, 1.0, 0.0).astype(jnp.float32)

    def select(table_all):
        return lax.dynamic_index_in_dim(table_all, pick, 0, keepdims=False)

    def into_slot(term):
        return slot_hot.reshape((-1,) + (1,) * term.ndim) * term[None]

    head_local = qkv_weight.shape[2] // HEAD_DIM
    width_local = qkv_weight.shape[2]

    def to_windows(values):
        return values.reshape(-1, WIN, WIN, head_local, HEAD_DIM).transpose(0, 3, 1, 2, 4)

    def from_windows(values):
        return values.transpose(0, 2, 3, 1, 4).reshape(full_rows, -1)

    gain_one = norm1_gain.astype(jnp.float32)
    gain_two = norm2_gain.astype(jnp.float32)
    table_h = offset_table(rel_pos_h)
    table_w = offset_table(rel_pos_w)
    a_qkv = select(qkv_down)
    b_qkv = select(qkv_up).reshape(RANK, -1)
    a_proj = select(proj_down)
    b_proj = select(proj_up)
    a_lin1 = select(lin1_down)
    b_lin2 = select(lin2_up)
    qkv_flat = qkv_weight.reshape(qkv_weight.shape[0], -1)
    x_local = tokens.astype(jnp.float32)
    normal_one, inv_one = norm_parts(x_local)
    xn1_local = (valid_local * (normal_one * gain_one + norm1_shift.astype(jnp.float32))).astype(
        jnp.bfloat16
    )
    xn1 = lax.all_gather(xn1_local, "tensor", axis=0, tiled=True)
    down_q = fast_dot(xn1, a_qkv)
    qkv = (
        fast_dot(xn1, qkv_flat)
        + qkv_bias.astype(jnp.float32).reshape(-1)
        + ADAPT * exact_dot(down_q, b_qkv)
    )
    qkv = qkv.astype(jnp.bfloat16).reshape(full_rows, 3, width_local)
    queries = to_windows(qkv[:, 0])
    key_win = to_windows(qkv[:, 1])
    value_win = to_windows(qkv[:, 2])
    win_count = queries.shape[0]
    tokens_win = WIN * WIN
    scores = window_scores(queries, key_win, table_h, table_w)
    row_max = jnp.max(scores, axis=-1, keepdims=True)
    exponent = jnp.exp(scores - row_max)
    row_total = jnp.sum(exponent, axis=-1, keepdims=True)
    log_total = row_max + jnp.log(row_total)
    probs = exponent / row_total
    attended = jnp.einsum(
        "nhqk,nhkc->nhqc",
        probs.astype(jnp.bfloat16),
        value_win.reshape(win_count, head_local, tokens_win, -1),
        preferred_element_type=jnp.float32,
    )
    att = from_windows(attended.reshape(queries.shape)).astype(jnp.bfloat16)
    down_p = fast_dot(att, a_proj)
    down_part = down_p
    branch_a = lax.psum_scatter(
        (fast_dot(att, proj_weight) + ADAPT * exact_dot(down_part, b_proj)).astype(jnp.bfloat16),
        "tensor",
        scatter_dimension=0,
        tiled=True,
    ).astype(jnp.float32)
    middle = x_local + valid_local * (branch_a + proj_bias.astype(jnp.float32))
    normal_two, inv_two = norm_parts(middle)
    xn2_local = (normal_two * gain_two + norm2_shift.astype(jnp.float32)).astype(jnp.bfloat16)
    xn2 = lax.all_gather(xn2_local, "tensor", axis=0, tiled=True)
    w_lin1, c_lin1, b_lin1, a_lin2, w_lin2 = (
        lin1_weight,
        lin1_bias,
        select(lin1_up),
        select(lin2_down),
        lin2_weight,
    )
    down_1 = fast_dot(xn2, a_lin1)
    hidden_pre = (
        fast_dot(xn2, w_lin1) + c_lin1.astype(jnp.float32) + ADAPT * exact_dot(down_1, b_lin1)
    )
    gelu_value, gelu_grad = jax.vjp(
        lambda values: jax.nn.gelu(values, approximate=False), hidden_pre
    )
    hidden_act = gelu_value.astype(jnp.bfloat16)
    down_2 = fast_dot(hidden_act, a_lin2)
    down_part = down_2
    branch_m = lax.psum_scatter(
        (fast_dot(hidden_act, w_lin2) + ADAPT * exact_dot(down_part, b_lin2)).astype(jnp.bfloat16),
        "tensor",
        scatter_dimension=0,
        tiled=True,
    ).astype(jnp.float32)
    output = (middle + valid_local * (branch_m + lin2_bias.astype(jnp.float32))).astype(
        jnp.bfloat16
    )
    dout_f = grad_out.astype(jnp.float32)
    dy2_local = (valid_local * dout_f).astype(jnp.bfloat16)
    dy2 = lax.all_gather(dy2_local, "tensor", axis=0, tiled=True)
    up2 = trans_dot(dy2, b_lin2)
    dact = trans_dot(dy2, w_lin2) + ADAPT * exact_dot(up2, a_lin2.T)
    dpre = gelu_grad(dact)[0].astype(jnp.bfloat16)
    up1 = trans_dot(dpre, b_lin1)
    grad_lin2_up_t = ADAPT * cross_dot(down_2, dy2)
    grad_lin2_down_t = ADAPT * cross_dot(hidden_act, up2)
    grad_lin1_up_t = ADAPT * cross_dot(down_1, dpre)
    grad_lin1_down_t = ADAPT * cross_dot(xn2, up1)
    up_part = up1
    dxn2 = lax.psum_scatter(
        (trans_dot(dpre, w_lin1) + ADAPT * exact_dot(up_part, a_lin1.T)).astype(jnp.bfloat16),
        "tensor",
        scatter_dimension=0,
        tiled=True,
    ).astype(jnp.float32)
    dmiddle = dout_f + norm_back(dxn2, normal_two, inv_two, gain_two)
    dya_local = (valid_local * dmiddle).astype(jnp.bfloat16)
    dya = lax.all_gather(dya_local, "tensor", axis=0, tiled=True)
    upp = trans_dot(dya, b_proj)
    datt = (trans_dot(dya, proj_weight) + ADAPT * exact_dot(upp, a_proj.T)).astype(jnp.bfloat16)
    grad_proj_up_t = ADAPT * cross_dot(down_p, dya)
    grad_proj_down_t = ADAPT * cross_dot(att, upp)
    dqueries, dkeys, dvalues = attention_back(
        queries, key_win, value_win, log_total, to_windows(datt), table_h, table_w
    )
    dqkv = jnp.stack(
        [from_windows(dqueries), from_windows(dkeys), from_windows(dvalues)], axis=1
    ).reshape(full_rows, -1)
    upq = trans_dot(dqkv, b_qkv)
    grad_qkv_up_t = (ADAPT * cross_dot(down_q, dqkv)).reshape(RANK, 3, -1)
    grad_qkv_down_t = ADAPT * cross_dot(xn1, upq)
    up_part = upq
    dxn1 = lax.psum_scatter(
        (trans_dot(dqkv, qkv_flat) + ADAPT * exact_dot(up_part, a_qkv.T)).astype(jnp.bfloat16),
        "tensor",
        scatter_dimension=0,
        tiled=True,
    ).astype(jnp.float32)
    grad_tokens = (dmiddle + norm_back(valid_local * dxn1, normal_one, inv_one, gain_one)).astype(
        jnp.bfloat16
    )
    grad_qkv_up, grad_proj_down, grad_lin1_up, grad_lin2_down = lax.psum(
        (
            into_slot(grad_qkv_up_t),
            into_slot(grad_proj_down_t),
            into_slot(grad_lin1_up_t),
            into_slot(grad_lin2_down_t),
        ),
        "dp",
    )
    grad_qkv_down, grad_proj_up, grad_lin1_down, grad_lin2_up = lax.psum(
        (
            into_slot(grad_qkv_down_t),
            into_slot(grad_proj_up_t),
            into_slot(grad_lin1_down_t),
            into_slot(grad_lin2_up_t),
        ),
        ("dp", "tensor"),
    )
    return (
        output,
        grad_tokens,
        grad_qkv_down,
        grad_qkv_up,
        grad_proj_down,
        grad_proj_up,
        grad_lin1_down,
        grad_lin1_up,
        grad_lin2_down,
        grad_lin2_up,
    )


def solution(mesh):
    placed = (
        P(("dp", "tensor"), None),
        P(("dp", "tensor"), None),
        P(),
        P(),
        P(),
        P(None, None, "tensor"),
        P(None, "tensor"),
        P(),
        P(),
        P("tensor", None),
        P(),
        P(),
        P(),
        P(None, "tensor"),
        P("tensor"),
        P("tensor", None),
        P(),
        P(),
        P(None, None, None, "tensor"),
        P(None, "tensor", None),
        P(),
        P(),
        P(None, None, "tensor"),
        P(None, "tensor", None),
        P(),
    )
    return jax.shard_map(
        on_device,
        mesh=mesh,
        in_specs=placed,
        out_specs=(
            P(("dp", "tensor"), None),
            P(("dp", "tensor"), None),
            P(),
            P(None, None, None, "tensor"),
            P(None, "tensor", None),
            P(),
            P(),
            P(None, None, "tensor"),
            P(None, "tensor", None),
            P(),
        ),
        check_vma=False,
    )
```

profile of v0, /device:TPU:0, one launch (start us, length us, event | category | flops | bytes accessed | tf_op | source)
XLA Modules:
  0.0 929.5 jit_solution(8334608292282891529)
XLA Ops:
  19.2 28.9 %all-gather.9.cloned.1.call-done = bf16[4,343,1280]{2,1,0:T(8,128)(2,1)} async-done(((bf16[1,343,1280]{2,1,0:T(8,128)(2,1)}), bf16[4,343,1280]{2,1,0:T(8,128)(2,1)}) %all-gather.9.cloned.1.call-update) | async-done | bytes 3512336 | tf_op jit(solution)/shard_map/all_gather | solution.py:205
  48.1 4.7 reshape.204
  56.0 5.7 fusion.149
  68.7 3.9 reshape_squeeze.10
  72.6 3.8 copy.99
  78.8 3.9 reshape_squeeze.9
  85.0 3.9 reshape_squeeze.11
  88.9 3.8 copy.109
  96.2 3.9 copy.98
  100.1 6.8 convolution_bitcast_fusion.2
  106.9 5.8 copy.101
  112.7 6.8 convolution_bitcast_fusion.1
  119.5 6.3 copy.105
  125.8 16.1 %add.258 = f32[7,4,14,14,14,14]{5,4,3,2,1,0:T(8,128)} broadcast(f32[7,4,14,14,14]{4,3,2,1,0:T(8,128)} %copy.105), dimensions={0,1,2,3,5} | broadcast | bytes 4609920 | tf_op jit(solution)/shard_map/add | solution.py:86
  141.9 26.9 %add.259 = f32[7,4,196,196]{3,2,1,0:T(8,128)} reshape(f32[7,4,14,14,14,14]{5,4,3,2,1,0:T(8,128)} %add.258) | data formatting | bytes 8605184 | tf_op jit(solution)/shard_map/add | solution.py:86
  168.8 6.8 copy.106
  175.6 16.6 %add.255 = f32[7,4,14,14,14,14]{5,4,3,2,1,0:T(8,128)} broadcast(f32[7,4,14,14,14]{4,3,2,1,0:T(8,128)} %copy.101), dimensions={0,1,2,3,4} | broadcast | bytes 4609920 | tf_op jit(solution)/shard_map/add | solution.py:86
  192.2 26.9 %add.256 = f32[7,4,196,196]{3,2,1,0:T(8,128)} reshape(f32[7,4,14,14,14,14]{5,4,3,2,1,0:T(8,128)} %add.255) | data formatting | bytes 8605184 | tf_op jit(solution)/shard_map/add | solution.py:86
  219.1 6.5 copy.102
  225.5 6.3 fusion.148
  236.4 3.9 copy.110
  248.9 5.7 fusion.13
  254.6 35.5 %fusion = bf16[344,1280]{1,0:T(8,128)(2,1)} fusion(bf16[1372,1280]{1,0:T(8,128)(2,1)} %fusion.13), kind=kCustom, calls=%all-reduce-scatter | all-reduce-scatter fusion | flops 1761281 | bytes 4393472
  293.5 6.1 concatenate
  306.8 33.4 %all-gather.13.cloned.1.call-done = bf16[4,343,1280]{2,1,0:T(8,128)(2,1)} async-done(((bf16[1,343,1280]{2,1,0:T(8,128)(2,1)}), bf16[4,343,1280]{2,1,0:T(8,128)(2,1)}) %all-gather.13.cloned.1.call-update) | async-done | bytes 3512336 | tf_op jit(solution)/shard_map/all_gather | solution.py:271
  340.2 4.7 reshape.208
  348.1 9.0 fusion.152
  357.2 15.9 %all-gather.11.cloned.1.call-done = bf16[4,343,1280]{2,1,0:T(8,128)(2,1)} async-done(((bf16[1,343,1280]{2,1,0:T(8,128)(2,1)}), bf16[4,343,1280]{2,1,0:T(8,128)(2,1)}) %all-gather.11.cloned.1.call-update) | async-done | bytes 3512336 | tf_op jit(solution)/shard_map/all_gather | solution.py:242
  373.1 4.8 reshape.206
  381.1 4.9 convolution_add_fusion
  386.0 22.5 %multiply_convert_fusion = (bf16[1372,1280]{1,0:T(8,128)(2,1)}, f32[1372,1280]{1,0:T(8,128)S(1)}, f32[1372,1280]{1,0:T(8,128)}) fusion(f32[1372,1280]{1,0:T(8,128)S(1)} %convolution_add_fusion, f32[1372,16]{0,1:T(8,128)S(1)} %fusion.81, bf16[8,16,1280]{2,1,0:T(8,128)(2,1)} %param.47, s32[]{:T(128)S(6)} %select_n.86), kind=kOutput, calls=%fused_computation.21 | convolution fusion | flops 454845440 | bytes 24715012 | tf_op jit(solution)/shard_map/dot_general | solution.py:30
  408.5 9.7 %add_convert_fusion = bf16[1372,1280]{1,0:T(8,128)(2,1)S(1)} fusion(f32[1372,1280]{1,0:T(8,128)S(1)} %get-tuple-element.31, f32[1372,1280]{1,0:T(8,128)S(1)} %bitcast.198, f32[1372,16]{0,1:T(8,128)S(1)} %fusion.71, f32[1372,1280]{1,0:T(8,128)} %get-tuple-element.47, bf16[8,1280,16]{1,2,0:T(8,128)(2,1)} %param.48, s32[]{:T(128)S(6)} %select_n.86), kind=kOutput, calls=%fused_computation.20 | convolution fusion | flops 365281280 | bytes 24735492 | tf_op jit(solution)/shard_map/dot_general | solution.py:30
  420.0 4.8 fusion.153
  424.8 6.0 fusion.11
  430.9 35.2 %fusion.2 = bf16[344,1280]{1,0:T(8,128)(2,1)} fusion(bf16[1372,1280]{1,0:T(8,128)(2,1)} %fusion.11), kind=kCustom, calls=%all-reduce-scatter.2 | all-reduce-scatter fusion | flops 1761281 | bytes 4393472
  469.0 6.7 concatenate.2
  478.9 4.1 fusion.62
  497.3 4.8 fusion.151
  502.1 6.5 fusion.12
  508.5 9.3 all-gather.15.cloned.1.call-done
  517.8 4.7 reshape.210
  522.5 4.3 convolution_multiply_fusion.11
  536.2 3.9 reshape.194
  540.1 3.8 copy.112
  544.0 5.2 fusion.55
  549.1 4.3 multiply_reduce_fusion
  559.1 5.2 copy.117
  564.3 3.9 copy.128
  568.2 3.6 stack_reshape.11
  574.0 3.9 copy.125
  577.9 3.6 stack_reshape.10
  583.8 4.5 copy.116
  588.3 26.1 %reshape.202 = f32[7,4,14,14,14,14]{5,4,3,2,1,0:T(8,128)} reshape(f32[7,4,196,196]{3,2,1,0:T(8,128)} %copy.117) | data formatting | bytes 8605184 | tf_op jit(solution)/shard_map/reshape | solution.py:121
  614.4 19.9 %fusion.144 = (f32[7,4,14,14,14]{4,3,2,1,0:T(8,128)}, f32[7,4,14,14,14]{4,3,2,1,0:T(8,128)}) fusion(f32[7,4,14,14,14,14]{5,4,3,2,1,0:T(8,128)} %reshape.202), kind=kLoop, calls=%fused_computation.232 | loop fusion | flops 1997632 | bytes 4917248 | tf_op jit(solution)/shard_map/reduce_sum | solution.py:123
  634.3 4.4 fusion.23
  638.7 3.6 fusion.58
  666.6 6.4 convolution_bitcast_fusion
  673.0 5.7 fusion.10
  678.7 68.8 %fusion.145 = (bf16[344,1280]{1,0:T(8,128)(2,1)}, bf16[344,1280]{1,0:T(8,128)(2,1)}) fusion(bf16[1372,1280]{1,0:T(8,128)(2,1)} %fusion.12, bf16[1372,1280]{1,0:T(8,128)(2,1)} %fusion.10), kind=kCustom, calls=%all-reduce-scatter.4 | all-reduce-scatter fusion | flops 3522561 | bytes 8786432
  753.5 6.1 concatenate.3
  759.6 6.1 concatenate.1
  768.0 5.6 fusion.45
  773.5 31.3 %all-reduce.14.cloned.1.call-done = (f32[8,1280,16]{1,2,0:T(8,128)}, f32[8,16,1280]{2,1,0:T(8,128)}, f32[8,1280,16]{1,2,0:T(8,128)}, f32[8,16,1280]{2,1,0:T(8,128)}) async-done(((f32[8,1280,16]{1,2,0:T(8,128)}, f32[8,16,1280]{2,1,0:T(8,128)}, f32[8,1280,16]{1,2,0:T(8,128)}, f32[8,16,1280]{2,1,0:T(8,128)}), (f32[8,1280,16]{1,2,0:T(8,128)}, f32[8,16,1280]{2,1,0:T(8,128)}, f32[8,1280,16]{1,2,0:T(8,128)}, ...) | async-done | bytes 2621456 | tf_op jit(solution)/shard_map/psum | solution.py:322
  804.8 107.7 %all-reduce.16.cloned.1.call-done = (f32[8,16,3,320]{3,1,2,0:T(8,128)}, f32[8,320,16]{1,2,0:T(8,128)}, f32[8,16,1280]{2,1,0:T(8,128)}, f32[8,1280,16]{1,2,0:T(8,128)}) async-done(((f32[8,16,3,320]{3,1,2,0:T(8,128)}, f32[8,320,16]{1,2,0:T(8,128)}, f32[8,16,1280]{2,1,0:T(8,128)}, f32[8,1280,16]{1,2,0:T(8,128)}), (f32[8,16,3,320]{3,1,2,0:T(8,128)}, f32[8,320,16]{1,2,0:T(8,128)}, f32[8,16,1280]{2,1,0:T(8,128)}, ...) | async-done | bytes 1966096 | tf_op jit(solution)/shard_map/psum | solution.py:313
  (260 shorter events, 141.6 us)
Async XLA Ops:
  7.2 373.8 %copy-start = (bf16[1280,1280]{1,0:T(8,128)(2,1)S(1)}, bf16[1280,1280]{1,0:T(8,128)(2,1)}, u32[]{:S(2)}) copy-start(bf16[1280,1280]{1,0:T(8,128)(2,1)} %param.38) | copy-start | bytes 9830404
  7.2 7.4 copy-start.63
  7.2 9.3 %copy-start.58 = (bf16[3,320]{1,0:T(4,128)(2,1)S(1)}, bf16[3,320]{1,0:T(4,128)(2,1)}, u32[]{:S(2)}) copy-start(bf16[3,320]{1,0:T(4,128)(2,1)} %param.31) | copy-start | bytes 5764
  7.2 11.1 %copy-start.61 = (bf16[27,80]{1,0:T(8,128)(2,1)S(1)}, bf16[27,80]{1,0:T(8,128)(2,1)}, u32[]{:S(2)}) copy-start(bf16[27,80]{1,0:T(8,128)(2,1)} %param.33) | copy-start | bytes 12964
  7.2 11.5 %copy-start.62 = (bf16[27,80]{1,0:T(8,128)(2,1)S(1)}, bf16[27,80]{1,0:T(8,128)(2,1)}, u32[]{:S(2)}) copy-start(bf16[27,80]{1,0:T(8,128)(2,1)} %param.32) | copy-start | bytes 12964
  7.2 40.8 %all-gather.9.cloned.1.call-start = ((), (), s32[]{:S(2)}) async-start(), calls=%async_computation | async-start | bytes 4403200 | tf_op jit(solution)/shard_map/all_gather | solution.py:205
  8.8 8.6 copy-start.49
  10.4 7.0 copy-start.51
  11.1 6.3 copy-start.47
  14.5 325.7 %all-gather.13.cloned.1.call-start = ((), (), s32[]{:S(2)}) async-start(), calls=%async_computation.2 | async-start | bytes 4403200 | tf_op jit(solution)/shard_map/all_gather | solution.py:271
  18.3 43.4 %copy-start.45 = (bf16[16,960]{1,0:T(8,128)(2,1)}, bf16[16,960]{1,0:T(8,128)(2,1)S(1)}, u32[]{:S(2)}) copy-start(bf16[16,960]{1,0:T(8,128)(2,1)S(1)} %reshape.189) | copy-start | bytes 92164
  18.7 93.9 %copy-start.40 = (bf16[14,14,80,1,1]{2,1,0,3,4:T(8,128)(2,1)}, bf16[14,14,80,1,1]{2,1,0,3,4:T(8,128)(2,1)S(1)}, u32[]{:S(2)}) copy-start(bf16[14,14,80,1,1]{2,1,0,3,4:T(8,128)(2,1)S(1)} %reshape.212) | copy-start | bytes 94084
  19.2 80.9 %copy-start.42 = (bf16[14,14,80,1,1]{2,1,0,3,4:T(8,128)(2,1)}, bf16[14,14,80,1,1]{2,1,0,3,4:T(8,128)(2,1)S(1)}, u32[]{:S(2)}) copy-start(bf16[14,14,80,1,1]{2,1,0,3,4:T(8,128)(2,1)S(1)} %reshape.211) | copy-start | bytes 94084
  52.8 3.2 copy-start.4
  55.9 5.8 copy-start.27
  254.6 37.5 %copy-start.53 = (bf16[1280]{0:T(1024)(128)(2,1)S(1)}, bf16[1280]{0:T(1024)(128)(2,1)}, u32[]{:S(2)}) copy-start(bf16[1280]{0:T(1024)(128)(2,1)} %param.35) | copy-start | bytes 7684
  254.6 37.6 %copy-start.54 = (bf16[1280]{0:T(1024)(128)(2,1)S(1)}, bf16[1280]{0:T(1024)(128)(2,1)}, u32[]{:S(2)}) copy-start(bf16[1280]{0:T(1024)(128)(2,1)} %param.36) | copy-start | bytes 7684
  254.6 37.6 %copy-start.55 = (bf16[1280]{0:T(1024)(128)(2,1)S(1)}, bf16[1280]{0:T(1024)(128)(2,1)}, u32[]{:S(2)}) copy-start(bf16[1280]{0:T(1024)(128)(2,1)} %param.37) | copy-start | bytes 7684
  254.6 37.6 %copy-start.59 = (u32[32]{0:T(128)S(1)}, u32[32]{0:T(128)}, u32[]{:S(2)}) copy-start(u32[32]{0:T(128)} %constant.209) | copy-start | bytes 388
  290.8 2.6 collective-permute-start
  299.5 4.5 copy-start.2
  299.5 4.5 copy-start.12
  299.5 4.5 copy-start.26
  306.0 67.1 %all-gather.11.cloned.1.call-start = ((), (), s32[]{:S(2)}) async-start(), calls=%async_computation.1 | async-start | bytes 4403200 | tf_op jit(solution)/shard_map/all_gather | solution.py:242
  306.7 211.1 %all-gather.15.cloned.1.call-start = ((), (), s32[]{:S(2)}) async-start(), calls=%async_computation.3 | async-start | bytes 4403200 | tf_op jit(solution)/shard_map/all_gather | solution.py:289
  348.1 60.4 %copy-start.37 = (f32[1372,16]{0,1:T(8,128)}, f32[1372,16]{0,1:T(8,128)S(1)}, u32[]{:S(2)}) copy-start(f32[1372,16]{0,1:T(8,128)S(1)} %fusion.71) | copy-start | bytes 263428
  377.9 3.2 copy-start.6
  381.1 4.9 copy-start.38
  381.1 27.4 %slice-start.2 = ((s8[7045120]{0:T(1024)(128)(4,1)}), s8[4194304]{0:T(1024)(128)(4,1)S(1)}, s32[]{:S(2)}) async-start(s8[7045120]{0:T(1024)(128)(4,1)} %bitcast.197), calls=%async_computation.8 | async-start | bytes 8388608
  386.0 22.5 %slice-start.3 = ((s8[7045120]{0:T(1024)(128)(4,1)}), s8[2850816]{0:T(1024)(128)(4,1)S(1)}, s32[]{:S(2)}) async-start(s8[7045120]{0:T(1024)(128)(4,1)} %bitcast.197), calls=%async_computation.9 | async-start | bytes 5701632
  418.2 6.7 copy-start.15
  466.8 2.2 collective-permute-start.2
  475.7 3.2 copy-start.3
  475.7 3.2 copy-start.13
  475.7 3.2 copy-start.23
  483.1 321.8 %all-reduce.14.cloned.1.call-start = ((), (), s32[]{:S(2)}) async-start(), calls=%async_computation.4 | async-start | bytes 5242880 | tf_op jit(solution)/shard_map/psum | solution.py:322
  483.3 4.5 copy-start.14
  522.5 4.3 copy-start.11
  533.9 10.1 %copy-start.44 = (f32[7,4,196]{2,1,0:T(4,128)S(1)}, f32[7,4,196]{2,1,0:T(4,128)}, u32[]{:S(2)}) copy-start(f32[7,4,196]{2,1,0:T(4,128)} %log_add_fusion) | copy-start | bytes 65860
  544.0 5.2 copy-start.22
  544.0 5.2 copy-start.25
  544.0 9.5 %slice-start = ((s8[5734400]{0:T(1024)(128)(4,1)}), s8[4194304]{0:T(1024)(128)(4,1)S(1)}, s32[]{:S(2)}) async-start(s8[5734400]{0:T(1024)(128)(4,1)} %bitcast.182), calls=%async_computation.6 | async-start | bytes 8388608
  549.1 4.3 slice-start.1
  614.4 19.9 %copy-start.41 = (bf16[14,14,80,1,1]{2,1,0,3,4:T(8,128)(2,1)S(1)}, bf16[14,14,80,1,1]{2,1,0,3,4:T(8,128)(2,1)}, u32[]{:S(2)}) copy-start(bf16[14,14,80,1,1]{2,1,0,3,4:T(8,128)(2,1)} %copy-done.40) | copy-start | bytes 94084
  634.3 4.4 copy-start.18
  634.3 4.5 copy-start.19
  634.3 4.5 copy-start.43
  647.6 4.5 copy-start.28
  650.0 5.0 copy-start.46
  652.1 3.4 copy-start.5
  657.6 7.3 copy-start.35
  659.2 5.7 copy-start.36
  666.3 246.2 %all-reduce.16.cloned.1.call-start = ((), (), s32[]{:S(2)}) async-start(), calls=%async_computation.5 | async-start | bytes 4194304 | tf_op jit(solution)/shard_map/psum | solution.py:313
  678.7 74.8 %copy-start.57 = (bf16[1280]{0:T(1024)(128)(2,1)S(1)}, bf16[1280]{0:T(1024)(128)(2,1)}, u32[]{:S(2)}) copy-start(bf16[1280]{0:T(1024)(128)(2,1)} %param.41) | copy-start | bytes 7684
  747.5 18.1 %copy-start.48 = (f32[1280]{0:T(1024)S(1)}, f32[1280]{0:T(1024)}, u32[]{:S(2)}) copy-start(f32[1280]{0:T(1024)} %copy-done.47) | copy-start | bytes 15364
  747.5 18.1 %copy-start.50 = (f32[343]{0:T(512)S(1)}, f32[343]{0:T(512)}, u32[]{:S(2)}) copy-start(f32[343]{0:T(512)} %copy-done.49) | copy-start | bytes 4120
  747.5 18.1 %copy-start.52 = (f32[343]{0:T(512)S(1)}, f32[343]{0:T(512)}, u32[]{:S(2)}) copy-start(f32[343]{0:T(512)} %copy-done.51) | copy-start | bytes 4120
  748.3 5.2 collective-permute-start.3
  750.3 9.2 collective-permute-start.1
  912.5 5.7 copy-start.32
  912.5 6.6 copy-start.31
  912.5 7.4 copy-start.34
  912.5 8.2 copy-start.33
  914.7 7.0 copy-start.30
  (14 other events, 31.9 us)
Sparse Core Ops, SparseCore 0:
  14.7 33.3 all-gather.8
  306.1 34.0 all-gather.12
  342.4 30.6 all-gather.10
  483.2 34.5 all-gather.14
  666.4 138.3 all-reduce.13
  810.3 102.1 all-reduce.15
where the time goes:
time: 941 us; the launch traced here: 930 us
  local copies, waits for them, and re-layouts  291 us (31%)
  waiting for transfers between devices  228 us (24%)
  matrix products  184 us (20%)
  blocking collectives  140 us (15%)
  other arithmetic  61.4 us (7%)
  between operations  17.9 us (2%)
    unnamed x3, blocking collectives  140 us
    psum x1, waiting for transfers between devices, on_device(): lax.psum((into_slot(grad_qkv_up_t), into_slot(grad_proj_down_t), into_slo...  108 us
    add x6, local copies, waits for them, and re-layouts, window_scores(): base_scores.reshape(win_count, head_count, WIN, WIN, WIN, WIN)  99.8 us
    unnamed x160, local copies, waits for them, and re-layouts  66.6 us
    dot_general x10, matrix products, exact_dot(): return jnp.dot(first_op, second_op.astype(jnp.float32), precision=HIGH)  62.1 us
    all_gather x1, waiting for transfers between devices, on_device(): dy2 = lax.all_gather(dy2_local, 'tensor', axis=0, tiled=True)  33.4 us
    reshape x2, local copies, waits for them, and re-layouts, attention_back(): dscore.astype(jnp.float32)  31.3 us
    psum x1, waiting for transfers between devices, on_device(): lax.psum((into_slot(grad_qkv_down_t), into_slot(grad_proj_up_t), into_slo...  31.3 us
  transfers between devices with their start and end apart: 10, of which 7 were waited for; matrix products, arithmetic and copies ran while one was open for 16% of the time, Pallas kernels for 0%

commit v1 on v0

--- a/solution.py
+++ b/solution.py
@@ -14,6 +14,19 @@
 HIGH = lax.Precision.HIGHEST
 ADAPT = 0.5
 EPS = 1e-06
+
+
+def gather_around(x, axis, dim):
+    ways = lax.axis_size(axis)
+    up = [(d, (d + 1) % ways) for d in range(ways)]
+    down = [(d, (d - 1) % ways) for d in range(ways)]
+    earlier, later = ([x], [x])
+    for _ in range(ways // 2):
+        earlier.append(lax.ppermute(earlier[-1], axis, up))
+    for _ in range((ways - 1) // 2):
+        later.append(lax.ppermute(later[-1], axis, down))
+    line = jnp.concatenate([*earlier[::-1], *later[1:]], axis=dim)
+    return jnp.roll(line, (lax.axis_index(axis) - ways // 2) * x.shape[dim], axis=dim)
 
 
 def fast_dot(first_op, second_op):
@@ -268,7 +281,7 @@
     )
     dout_f = grad_out.astype(jnp.float32)
     dy2_local = (valid_local * dout_f).astype(jnp.bfloat16)
-    dy2 = lax.all_gather(dy2_local, "tensor", axis=0, tiled=True)
+    dy2 = gather_around(dy2_local, "tensor", 0)
     up2 = trans_dot(dy2, b_lin2)
     dact = trans_dot(dy2, w_lin2) + ADAPT * exact_dot(up2, a_lin2.T)
     dpre = gelu_grad(dact)[0].astype(jnp.bfloat16)

time: 941 us -> 983 us (1.045)
  local copies, waits for them, and re-layouts: 291 us -> 330 us
  waiting for transfers between devices: 228 us -> 210 us
  starting transfers between devices: 8.19 us -> 23.5 us
    concatenate x0 -> x1, local copies, waits for them, and re-layouts: none -> 42.9 us  [gather_around(): jnp.roll(line, (lax.axis_index(axis) - ways // 2) * x.shape[dim], axis=dim)]
    ppermute x0 -> x3, waiting for transfers between devices: none -> 35.2 us  [the longest x2 35.2 us: gather_around(): earlier.append(lax.ppermute(earlier[-1], axis, up))]
    all_gather x1 -> x0, waiting for transfers between devices: 33.4 us -> none  [on_device(): dy2 = lax.all_gather(dy2_local, 'tensor', axis=0, tiled=True)]
    all_gather x1, waiting for transfers between devices: 15.9 us -> 0.01 us  [on_device(): xn2 = lax.all_gather(xn2_local, 'tensor', axis=0, tiled=True)]
    ppermute x0 -> x3, starting transfers between devices: none -> 15.4 us  [the longest x2 15.3 us: gather_around(): earlier.append(lax.ppermute(earlier[-1], axis, up))]
    unnamed x160 -> x169, local copies, waits for them, and re-layouts: 66.6 us -> 62.7 us
  transfers between devices with their start and end apart: 10 -> 12, of which waited for: 7 -> 7; matrix products, arithmetic and copies ran while one was open for 16% -> 19% of each run, Pallas kernels for 0% -> 0%
where the time goes in v1:
time: 983 us; the launch traced here: 970 us
  local copies, waits for them, and re-layouts  330 us (34%)
  waiting for transfers between devices  210 us (21%)
  matrix products  186 us (19%)
  blocking collectives  141 us (14%)
  other arithmetic  62.6 us (6%)
  starting transfers between devices  23.5 us (2%)
  between operations  17.5 us (2%)
    unnamed x3, blocking collectives  141 us
    psum x1, waiting for transfers between devices, on_device(): lax.psum((into_slot(grad_qkv_up_t), into_slot(grad_proj_down_t), into_slo...  108 us
    add x6, local copies, waits for them, and re-layouts, window_scores(): base_scores.reshape(win_count, head_count, WIN, WIN, WIN, WIN)  99.7 us
    unnamed x169, local copies, waits for them, and re-layouts  62.7 us
    dot_general x10, matrix products, exact_dot(): return jnp.dot(first_op, second_op.astype(jnp.float32), precision=HIGH)  58.1 us
    concatenate x1, local copies, waits for them, and re-layouts, gather_around(): jnp.roll(line, (lax.axis_index(axis) - ways // 2) * x.shape[dim], axis=dim)  42.9 us
    ppermute x2, waiting for transfers between devices, gather_around(): earlier.append(lax.ppermute(earlier[-1], axis, up))  35.2 us
    dot_general x8, matrix products, trans_dot(): lax.dot_general(first_op, second_op, (((1,), (1,)), ((), ())), preferred_...  34 us
  transfers between devices with their start and end apart: 12, of which 7 were waited for; matrix products, arithmetic and copies ran while one was open for 19% of the time, Pallas kernels for 0%

profile of v1, /device:TPU:0, one launch (start us, length us, event | category | flops | bytes accessed | tf_op | source)
XLA Modules:
  0.0 970.3 jit_solution(6587987041403573618)
XLA Ops:
  19.1 29.0 %all-gather.7.cloned.1.call-done = bf16[4,343,1280]{2,1,0:T(8,128)(2,1)} async-done(((bf16[1,343,1280]{2,1,0:T(8,128)(2,1)}), bf16[4,343,1280]{2,1,0:T(8,128)(2,1)}) %all-gather.7.cloned.1.call-update) | async-done | bytes 3512336 | tf_op jit(solution)/shard_map/all_gather | solution.py:218
  48.1 4.7 reshape.204
  56.0 5.7 fusion.156
  68.7 3.9 reshape_squeeze.10
  72.6 3.8 copy.99
  78.7 3.9 reshape_squeeze.9
  85.0 3.9 reshape_squeeze.11
  88.9 3.8 copy.109
  96.1 3.9 copy.98
  100.0 6.8 convolution_bitcast_fusion.2
  106.8 5.7 copy.101
  112.6 6.8 convolution_bitcast_fusion.1
  119.4 6.3 copy.105
  125.7 16.1 %add.269 = f32[7,4,14,14,14,14]{5,4,3,2,1,0:T(8,128)} broadcast(f32[7,4,14,14,14]{4,3,2,1,0:T(8,128)} %copy.105), dimensions={0,1,2,3,5} | broadcast | bytes 4609920 | tf_op jit(solution)/shard_map/add | solution.py:99
  141.8 26.9 %add.270 = f32[7,4,196,196]{3,2,1,0:T(8,128)} reshape(f32[7,4,14,14,14,14]{5,4,3,2,1,0:T(8,128)} %add.269) | data formatting | bytes 8605184 | tf_op jit(solution)/shard_map/add | solution.py:99
  168.7 6.9 copy.106
  175.6 16.6 %add.266 = f32[7,4,14,14,14,14]{5,4,3,2,1,0:T(8,128)} broadcast(f32[7,4,14,14,14]{4,3,2,1,0:T(8,128)} %copy.101), dimensions={0,1,2,3,4} | broadcast | bytes 4609920 | tf_op jit(solution)/shard_map/add | solution.py:99
  192.1 26.9 %add.267 = f32[7,4,196,196]{3,2,1,0:T(8,128)} reshape(f32[7,4,14,14,14,14]{5,4,3,2,1,0:T(8,128)} %add.266) | data formatting | bytes 8605184 | tf_op jit(solution)/shard_map/add | solution.py:99
  219.0 6.4 copy.102
  225.4 6.3 fusion.155
  237.0 3.9 copy.110
  249.5 5.8 fusion.12
  255.3 35.5 %fusion = bf16[344,1280]{1,0:T(8,128)(2,1)} fusion(bf16[1372,1280]{1,0:T(8,128)(2,1)} %fusion.12), kind=kCustom, calls=%all-reduce-scatter | all-reduce-scatter fusion | flops 1761281 | bytes 4393472
  294.1 6.0 concatenate.7
  309.1 19.4 %collective-permute-done = bf16[343,1280]{1,0:T(8,128)(2,1)} collective-permute-done((bf16[343,1280]{1,0:T(8,128)(2,1)}, bf16[343,1280]{1,0:T(8,128)(2,1)}, u32[]{:S(2)}, u32[]{:S(2)}) %collective-permute-start) | collective-permute-done | bytes 878112 | tf_op jit(solution)/shard_map/ppermute | solution.py:25
  328.5 12.9 %collective-permute-start.1 = (bf16[343,1280]{1,0:T(8,128)(2,1)}, bf16[343,1280]{1,0:T(8,128)(2,1)}, u32[]{:S(2)}, u32[]{:S(2)}) collective-permute-start(bf16[343,1280]{1,0:T(8,128)(2,1)} %collective-permute-done), channel_id=1, source_target_pairs={{0,1},{1,2},{2,3},{3,0},{4,5},{5,6},{6,7},{7,4},{8,9},{9,10},{10,1... | collective-permute-start | bytes 2634248 | tf_op jit(solution)/shard_map/ppermute | solution.py:25
  341.5 15.8 %collective-permute-done.1 = bf16[343,1280]{1,0:T(8,128)(2,1)} collective-permute-done((bf16[343,1280]{1,0:T(8,128)(2,1)}, bf16[343,1280]{1,0:T(8,128)(2,1)}, u32[]{:S(2)}, u32[]{:S(2)}) %collective-permute-start.1) | collective-permute-done | bytes 878112 | tf_op jit(solution)/shard_map/ppermute | solution.py:25
  357.3 42.9 %concatenate.6 = bf16[2744,1280]{1,0:T(8,128)(2,1)} concatenate(bf16[343,1280]{1,0:T(8,128)(2,1)} %collective-permute-done.1, bf16[343,1280]{1,0:T(8,128)(2,1)} %collective-permute-done, bf16[343,1280]{1,0:T(8,128)(2,1)} %get-tuple-element.37, bf16[343,1280]{1,0:T(8,128)(2,1)} %collective-permute-done.2, bf16[343,1280]{1,0:T(8,128)(2,1)} %collective-permute-done.1, ...), dimensions={0} | concatenate | bytes 14049280 | tf_op jit(solution)/shard_map/jit(_roll_dynamic)/concatenate | solution.py:29
  403.2 6.6 convolution_multiply_fusion.2
  409.8 4.7 reshape.206
  417.8 4.8 convolution_add_fusion.1
  422.6 21.5 %multiply_convert_fusion = (bf16[1372,1280]{1,0:T(8,128)(2,1)}, f32[1372,1280]{1,0:T(8,128)}, f32[1372,1280]{1,0:T(8,128)}) fusion(f32[1372,1280]{1,0:T(8,128)S(1)} %convolution_add_fusion.1, f32[1372,16]{0,1:T(8,128)S(1)} %fusion.86, bf16[8,16,1280]{2,1,0:T(8,128)(2,1)} %param.47, s32[]{:T(128)S(6)} %select_n.98), kind=kOutput, calls=%fused_computation.21 | convolution fusion | flops 454845440 | bytes 24715012 | tf_op jit(solution)/shard_map/dot_general | solution.py:43
  444.1 12.8 %add_convert_fusion = bf16[1372,1280]{1,0:T(8,128)(2,1)} fusion(f32[1372,1280]{1,0:T(8,128)} %get-tuple-element.31, f32[1372,1280]{1,0:T(8,128)S(1)} %bitcast.182, bf16[1280,1280]{1,0:T(8,128)(2,1)} %param.40, f32[1372,1280]{1,0:T(8,128)} %get-tuple-element.47, bf16[2744,1280]{1,0:T(8,128)(2,1)} %concatenate.6, s32[]{:T(128)S(6)} %select_n.100), kind=kOutput, calls=%fused_computation.20 | convolution fusion | flops 4522112000 | bytes 31426564 | tf_op jit(solution)/shard_map/dot_general | solution.py:37
  460.1 4.8 fusion.159
  464.9 6.0 fusion.10
  470.9 36.2 %fusion.2 = bf16[344,1280]{1,0:T(8,128)(2,1)} fusion(bf16[1372,1280]{1,0:T(8,128)(2,1)} %fusion.10), kind=kCustom, calls=%all-reduce-scatter.2 | all-reduce-scatter fusion | flops 1761281 | bytes 4393472
  510.1 6.8 concatenate.9
  520.1 4.1 fusion.69
  530.1 4.5 fusion.37
  541.0 4.8 fusion.158
  545.8 6.5 fusion.11
  552.3 6.7 all-gather.11.cloned.1.call-done
  559.0 4.7 reshape.208
  563.7 4.3 convolution_multiply_fusion.10
  577.4 3.9 reshape.194
  581.3 3.8 copy.112
  585.2 5.1 fusion.62
  590.3 4.3 multiply_reduce_fusion
  600.3 5.2 copy.117
  605.5 3.9 copy.128
  615.3 3.9 copy.125
  625.0 4.5 copy.116
  629.5 26.1 %reshape.202 = f32[7,4,14,14,14,14]{5,4,3,2,1,0:T(8,128)} reshape(f32[7,4,196,196]{3,2,1,0:T(8,128)} %copy.117) | data formatting | bytes 8605184 | tf_op jit(solution)/shard_map/reshape | solution.py:134
  655.6 19.9 %fusion.151 = (f32[7,4,14,14,14]{4,3,2,1,0:T(8,128)}, f32[7,4,14,14,14]{4,3,2,1,0:T(8,128)}) fusion(f32[7,4,14,14,14,14]{5,4,3,2,1,0:T(8,128)} %reshape.202), kind=kLoop, calls=%fused_computation.237 | loop fusion | flops 1997632 | bytes 4917248 | tf_op jit(solution)/shard_map/reduce_sum | solution.py:136
  675.5 4.4 fusion.22
  680.0 3.6 fusion.65
  707.8 6.4 convolution_bitcast_fusion
  714.2 5.7 fusion.9
  719.9 68.8 %fusion.152 = (bf16[344,1280]{1,0:T(8,128)(2,1)}, bf16[344,1280]{1,0:T(8,128)(2,1)}) fusion(bf16[1372,1280]{1,0:T(8,128)(2,1)} %fusion.11, bf16[1372,1280]{1,0:T(8,128)(2,1)} %fusion.9), kind=kCustom, calls=%all-reduce-scatter.4 | all-reduce-scatter fusion | flops 3522561 | bytes 8786432
  794.6 6.0 concatenate.10
  800.7 6.0 concatenate.8
  809.0 5.6 fusion.52
  814.6 31.3 %all-reduce.14.cloned.1.call-done = (f32[8,1280,16]{1,2,0:T(8,128)}, f32[8,16,1280]{2,1,0:T(8,128)}, f32[8,1280,16]{1,2,0:T(8,128)}, f32[8,16,1280]{2,1,0:T(8,128)}) async-done(((f32[8,1280,16]{1,2,0:T(8,128)}, f32[8,16,1280]{2,1,0:T(8,128)}, f32[8,1280,16]{1,2,0:T(8,128)}, f32[8,16,1280]{2,1,0:T(8,128)}), (f32[8,1280,16]{1,2,0:T(8,128)}, f32[8,16,1280]{2,1,0:T(8,128)}, f32[8,1280,16]{1,2,0:T(8,128)}, ...) | async-done | bytes 2621456 | tf_op jit(solution)/shard_map/psum | solution.py:335
  845.9 107.7 %all-reduce.16.cloned.1.call-done = (f32[8,16,3,320]{3,1,2,0:T(8,128)}, f32[8,320,16]{1,2,0:T(8,128)}, f32[8,16,1280]{2,1,0:T(8,128)}, f32[8,1280,16]{1,2,0:T(8,128)}) async-done(((f32[8,16,3,320]{3,1,2,0:T(8,128)}, f32[8,320,16]{1,2,0:T(8,128)}, f32[8,16,1280]{2,1,0:T(8,128)}, f32[8,1280,16]{1,2,0:T(8,128)}), (f32[8,16,3,320]{3,1,2,0:T(8,128)}, f32[8,320,16]{1,2,0:T(8,128)}, f32[8,16,1280]{2,1,0:T(8,128)}, ...) | async-done | bytes 1966096 | tf_op jit(solution)/shard_map/psum | solution.py:326
  (273 shorter events, 150.3 us)
Async XLA Ops:
  7.2 410.5 %copy-start = (bf16[1280,1280]{1,0:T(8,128)(2,1)S(1)}, bf16[1280,1280]{1,0:T(8,128)(2,1)}, u32[]{:S(2)}) copy-start(bf16[1280,1280]{1,0:T(8,128)(2,1)} %param.38) | copy-start | bytes 9830404
  7.2 7.4 copy-start.68
  7.2 9.3 copy-start.63
  7.2 11.0 %copy-start.66 = (bf16[27,80]{1,0:T(8,128)(2,1)S(1)}, bf16[27,80]{1,0:T(8,128)(2,1)}, u32[]{:S(2)}) copy-start(bf16[27,80]{1,0:T(8,128)(2,1)} %param.33) | copy-start | bytes 12964
  7.2 11.4 %copy-start.67 = (bf16[27,80]{1,0:T(8,128)(2,1)S(1)}, bf16[27,80]{1,0:T(8,128)(2,1)}, u32[]{:S(2)}) copy-start(bf16[27,80]{1,0:T(8,128)(2,1)} %param.32) | copy-start | bytes 12964
  7.2 40.8 %all-gather.7.cloned.1.call-start = ((), (), s32[]{:S(2)}) async-start(), calls=%async_computation | async-start | bytes 4403200 | tf_op jit(solution)/shard_map/all_gather | solution.py:218
  8.8 8.5 copy-start.52
  10.4 6.9 copy-start.55
  11.1 6.2 copy-start.47
  11.9 292.8 %copy-start.45 = (f32[343]{0:T(512)}, f32[343]{0:T(512)S(1)}, u32[]{:S(2)}) copy-start(f32[343]{0:T(512)S(1)} %fusion.148) | copy-start | bytes 4120
  14.6 395.3 %all-gather.9.cloned.1.call-start = ((), (), s32[]{:S(2)}) async-start(), calls=%async_computation.1 | async-start | bytes 4403200 | tf_op jit(solution)/shard_map/all_gather | solution.py:255
  18.3 43.5 %copy-start.42 = (bf16[16,960]{1,0:T(8,128)(2,1)}, bf16[16,960]{1,0:T(8,128)(2,1)S(1)}, u32[]{:S(2)}) copy-start(bf16[16,960]{1,0:T(8,128)(2,1)S(1)} %reshape.189) | copy-start | bytes 92164
  18.7 93.9 %copy-start.37 = (bf16[14,14,80,1,1]{2,1,0,3,4:T(8,128)(2,1)}, bf16[14,14,80,1,1]{2,1,0,3,4:T(8,128)(2,1)S(1)}, u32[]{:S(2)}) copy-start(bf16[14,14,80,1,1]{2,1,0,3,4:T(8,128)(2,1)S(1)} %reshape.210) | copy-start | bytes 94084
  19.1 80.9 %copy-start.39 = (bf16[14,14,80,1,1]{2,1,0,3,4:T(8,128)(2,1)}, bf16[14,14,80,1,1]{2,1,0,3,4:T(8,128)(2,1)S(1)}, u32[]{:S(2)}) copy-start(bf16[14,14,80,1,1]{2,1,0,3,4:T(8,128)(2,1)S(1)} %reshape.209) | copy-start | bytes 94084
  55.9 5.8 copy-start.25
  255.3 37.5 %copy-start.58 = (bf16[1280]{0:T(1024)(128)(2,1)S(1)}, bf16[1280]{0:T(1024)(128)(2,1)}, u32[]{:S(2)}) copy-start(bf16[1280]{0:T(1024)(128)(2,1)} %param.35) | copy-start | bytes 7684
  255.3 37.6 %copy-start.59 = (bf16[1280]{0:T(1024)(128)(2,1)S(1)}, bf16[1280]{0:T(1024)(128)(2,1)}, u32[]{:S(2)}) copy-start(bf16[1280]{0:T(1024)(128)(2,1)} %param.36) | copy-start | bytes 7684
  255.3 37.6 %copy-start.60 = (bf16[1280]{0:T(1024)(128)(2,1)S(1)}, bf16[1280]{0:T(1024)(128)(2,1)}, u32[]{:S(2)}) copy-start(bf16[1280]{0:T(1024)(128)(2,1)} %param.37) | copy-start | bytes 7684
  255.3 37.6 %copy-start.64 = (u32[32]{0:T(128)S(1)}, u32[32]{0:T(128)}, u32[]{:S(2)}) copy-start(u32[32]{0:T(128)} %constant.229) | copy-start | bytes 388
  291.5 2.6 collective-permute-start.3
  292.8 13.8 %copy-start.49 = (f32[1280]{0:T(1024)}, f32[1280]{0:T(1024)S(1)}, u32[]{:S(2)}) copy-start(f32[1280]{0:T(1024)S(1)} %convert_element_type.173) | copy-start | bytes 15364
  300.1 4.5 copy-start.2
  300.2 4.5 copy-start.10
  300.2 4.6 copy-start.24
  302.4 39.1 %copy-start.61 = (bf16[1280]{0:T(1024)(128)(2,1)S(1)}, bf16[1280]{0:T(1024)(128)(2,1)}, u32[]{:S(2)}) copy-start(bf16[1280]{0:T(1024)(128)(2,1)} %param.39) | copy-start | bytes 7684
  304.7 52.6 %copy-start.54 = (f32[343]{0:T(512)}, f32[343]{0:T(512)S(1)}, u32[]{:S(2)}) copy-start(f32[343]{0:T(512)S(1)} %add_rsqrt_fusion) | copy-start | bytes 4120
  306.7 252.3 %all-gather.11.cloned.1.call-start = ((), (), s32[]{:S(2)}) async-start(), calls=%async_computation.2 | async-start | bytes 4403200 | tf_op jit(solution)/shard_map/all_gather | solution.py:302
  306.7 21.8 %collective-permute-start = (bf16[343,1280]{1,0:T(8,128)(2,1)}, bf16[343,1280]{1,0:T(8,128)(2,1)}, u32[]{:S(2)}, u32[]{:S(2)}) collective-permute-start(bf16[343,1280]{1,0:T(8,128)(2,1)} %get-tuple-element.37), channel_id=1, source_target_pairs={{0,1},{1,2},{2,3},{3,0},{4,5},{5,6},{6,7},{7,4},{8,9},{9,10},{10,1... | collective-permute-start | bytes 2634248 | tf_op jit(solution)/shard_map/ppermute | solution.py:25
  309.1 32.3 %collective-permute-start.2 = (bf16[343,1280]{1,0:T(8,128)(2,1)}, bf16[343,1280]{1,0:T(8,128)(2,1)}, u32[]{:S(2)}, u32[]{:S(2)}) collective-permute-start(bf16[343,1280]{1,0:T(8,128)(2,1)} %get-tuple-element.37), channel_id=1, source_target_pairs={{0,3},{1,0},{2,1},{3,2},{4,7},{5,4},{6,5},{7,6},{8,11},{9,8},{10,9... | collective-permute-start | bytes 2634248 | tf_op jit(solution)/shard_map/ppermute | solution.py:27
  328.5 28.7 %collective-permute-start.1 = (bf16[343,1280]{1,0:T(8,128)(2,1)}, bf16[343,1280]{1,0:T(8,128)(2,1)}, u32[]{:S(2)}, u32[]{:S(2)}) collective-permute-start(bf16[343,1280]{1,0:T(8,128)(2,1)} %collective-permute-done), channel_id=1, source_target_pairs={{0,1},{1,2},{2,3},{3,0},{4,5},{5,6},{6,7},{7,4},{8,9},{9,10},{10,1... | collective-permute-start | bytes 2634248 | tf_op jit(solution)/shard_map/ppermute | solution.py:25
  417.7 4.8 copy-start.35
  417.7 26.3 %slice-start.2 = ((s8[7045120]{0:T(1024)(128)(4,1)}), s8[4194304]{0:T(1024)(128)(4,1)S(1)}, s32[]{:S(2)}) async-start(s8[7045120]{0:T(1024)(128)(4,1)} %bitcast.181), calls=%async_computation.7 | async-start | bytes 8388608
  422.5 21.5 %slice-start.3 = ((s8[7045120]{0:T(1024)(128)(4,1)}), s8[2850816]{0:T(1024)(128)(4,1)S(1)}, s32[]{:S(2)}) async-start(s8[7045120]{0:T(1024)(128)(4,1)} %bitcast.181), calls=%async_computation.8 | async-start | bytes 5701632
  507.9 2.2 collective-permute-start.5
  524.2 321.7 %all-reduce.14.cloned.1.call-start = ((), (), s32[]{:S(2)}) async-start(), calls=%async_computation.3 | async-start | bytes 5242880 | tf_op jit(solution)/shard_map/psum | solution.py:335
  527.0 7.7 copy-start.12
  563.7 4.3 copy-start.9
  575.1 10.0 %copy-start.41 = (f32[7,4,196]{2,1,0:T(4,128)S(1)}, f32[7,4,196]{2,1,0:T(4,128)}, u32[]{:S(2)}) copy-start(f32[7,4,196]{2,1,0:T(4,128)} %log_add_fusion) | copy-start | bytes 65860
  585.2 5.2 copy-start.20
  585.2 5.2 copy-start.23
  585.2 9.4 slice-start
  590.3 4.3 slice-start.1
  655.6 19.9 %copy-start.38 = (bf16[14,14,80,1,1]{2,1,0,3,4:T(8,128)(2,1)S(1)}, bf16[14,14,80,1,1]{2,1,0,3,4:T(8,128)(2,1)}, u32[]{:S(2)}) copy-start(bf16[14,14,80,1,1]{2,1,0,3,4:T(8,128)(2,1)} %copy-done.37) | copy-start | bytes 94084
  675.5 4.4 copy-start.16
  675.5 4.5 copy-start.17
  675.5 4.5 copy-start.40
  688.8 4.4 copy-start.26
  691.2 5.0 copy-start.43
  696.6 4.7 copy-start.57
  698.8 7.3 copy-start.33
  700.4 5.7 copy-start.34
  707.5 246.1 %all-reduce.16.cloned.1.call-start = ((), (), s32[]{:S(2)}) async-start(), calls=%async_computation.4 | async-start | bytes 4194304 | tf_op jit(solution)/shard_map/psum | solution.py:326
  719.9 74.7 %copy-start.62 = (bf16[1280]{0:T(1024)(128)(2,1)S(1)}, bf16[1280]{0:T(1024)(128)(2,1)}, u32[]{:S(2)}) copy-start(bf16[1280]{0:T(1024)(128)(2,1)} %param.41) | copy-start | bytes 7684
  788.7 18.0 %copy-start.46 = (f32[343]{0:T(512)S(1)}, f32[343]{0:T(512)}, u32[]{:S(2)}) copy-start(f32[343]{0:T(512)} %copy-done.45) | copy-start | bytes 4120
  788.7 18.0 %copy-start.48 = (f32[1280]{0:T(1024)S(1)}, f32[1280]{0:T(1024)}, u32[]{:S(2)}) copy-start(f32[1280]{0:T(1024)} %copy-done.47) | copy-start | bytes 15364
  788.7 18.0 %copy-start.53 = (f32[343]{0:T(512)S(1)}, f32[343]{0:T(512)}, u32[]{:S(2)}) copy-start(f32[343]{0:T(512)} %copy-done.52) | copy-start | bytes 4120
  788.7 18.0 %copy-start.56 = (f32[343]{0:T(512)S(1)}, f32[343]{0:T(512)}, u32[]{:S(2)}) copy-start(f32[343]{0:T(512)} %copy-done.55) | copy-start | bytes 4120
  789.5 5.1 collective-permute-start.6
  791.5 9.2 collective-permute-start.4
  953.6 5.7 copy-start.30
  953.6 6.6 copy-start.29
  953.6 7.4 copy-start.32
  953.6 8.2 copy-start.31
  955.8 7.0 copy-start.28
  (21 other events, 53.2 us)
Sparse Core Ops, SparseCore 0:
  14.7 33.3 all-gather.6
  306.8 48.8 all-gather.8
  524.4 34.5 all-gather.10
  707.6 138.2 all-reduce.13
  851.4 102.1 all-reduce.15
